TPU v7x, 32 devices: a whole 2x2x4 slice. The times are simulated.
32 devices in a mesh: ctx: 16 (over z, x, core), head: 2 (over y).
Axes of the slice: x: 2, y: 2, z: 4, core: 2. Of those that a mesh axis runs over, the one named last changes fastest.
Arguments:
- queries: bfloat16 [4096, 6144], P(('ctx', 'head')), may hold values from -32 to 32
- keys: bfloat16 [4096, 6144], P(('ctx', 'head')), may hold values from -12 to 12
- values: bfloat16 [4096, 6144], P(('ctx', 'head')), may hold values from -6 to 6
- cache_keys: bfloat16 [8192, 6144], P('ctx', 'head'), may hold values from -6 to 6
- cache_values: bfloat16 [8192, 6144], P('ctx', 'head'), may hold values from -6 to 6
- pattern: int32 [32, 4], replicated, may hold values from 0 to 63, as said below
- reached: int32 [32], replicated, may hold values from 1 to 4, as said below
- gate: float32 [6144], replicated, may hold values from 0.5 to 2
Outputs:
- mixed: bfloat16 [4096, 6144], P(('ctx', 'head'))
Inputs may be any that keep to these rules, and one draw needn't show every extreme that they name: `pattern`: every entry of row g names a cached tile of ctx index g // 2 - 1, g // 2 or g // 2 + 1, where ctx index c holds cached tiles c * 4 to (c + 1) * 4 - 1. Only the first reached[g] entries of row g of pattern are used.
All inputs are finite; a program needn't handle non-finite values.
Results may differ from a plain program's by a relative error of at most 0.011.
Values may be sent and summed in bfloat16 or wider, within the bound.
A program may use at most 128 MiB of HBM per device.

v0:
```python
import jax
import jax.numpy as jnp
from jax import lax
from jax.sharding import PartitionSpec as P

HD = 128
TILE = 128
REACH = 4


NEGATIVE = -1e30


def with_halo(block, sides, width):
    for axis, dim in sides:
        count = lax.axis_size(axis)
        forward = [(i, i + 1) for i in range(count - 1)]
        backward = [(target, source) for source, target in forward]
        low = lax.ppermute(
            lax.slice_in_dim(block, block.shape[dim] - width, None, axis=dim), axis, forward
        )
        high = lax.ppermute(lax.slice_in_dim(block, 0, width, axis=dim), axis, backward)
        block = jnp.concatenate([low, block, high], axis=dim)
    return block


def tile_attend(q_tile, key_blocks, value_blocks, usable_keys):
    scores = jnp.einsum(
        "qhd,nkhd->hqnk", q_tile, key_blocks, preferred_element_type=jnp.float32
    ) * q_tile.shape[2] ** (-0.5)
    keep_mask = usable_keys[None, None, :, None]
    scores = jnp.where(keep_mask, scores, NEGATIVE)
    row_peak = jnp.max(scores, axis=(2, 3))
    expos = jnp.exp(scores - row_peak[:, :, None, None])
    row_total = jnp.sum(expos, axis=(2, 3))
    weights = expos.astype(jnp.bfloat16)
    summed = jnp.einsum("hqnk,nkhd->qhd", weights, value_blocks, preferred_element_type=jnp.float32)
    return (summed, row_peak, row_total)


def finish(portions):
    overall_peak = portions[0][1]
    numerator = 0.0
    denominator = 0.0
    for portion in portions:
        factor = jnp.exp(portion[1] - overall_peak)
        denominator = denominator + factor * portion[2]
        numerator = numerator + portion[0] * jnp.transpose(factor, (0, 2, 1))[..., None]
    return numerator / jnp.transpose(denominator, (0, 2, 1))[..., None]


def local(queries, keys, values, cache_keys, cache_values, pattern, reached, gate):
    local_q, local_k, local_v = (
        lax.all_to_all(queries, "head", split_axis=1, concat_axis=0, tiled=True),
        lax.all_to_all(keys, "head", split_axis=1, concat_axis=0, tiled=True),
        lax.all_to_all(values, "head", split_axis=1, concat_axis=0, tiled=True),
    )
    rows = local_q.shape[0]
    width = local_q.shape[1]
    heads_here = width // HD
    tiles_here = rows // TILE
    ctx_count = lax.axis_size("ctx")
    ctx_index = lax.axis_index("ctx")
    all_tiles = ctx_count * tiles_here
    first_tile = ctx_index * tiles_here
    cache_tiles = cache_keys.shape[0] // TILE
    rim_blocks = with_halo(jnp.stack([local_k, local_v]), (("ctx", 1),), 2 * TILE)
    tile_ids = first_tile + jnp.arange(tiles_here, dtype=jnp.int32)
    near_ids = tile_ids[:, None] + jnp.arange(-2, 3, dtype=jnp.int32)[None, :]
    group_valid = (near_ids >= 0) & (near_ids < all_tiles)
    own_pattern = lax.dynamic_slice_in_dim(pattern, first_tile, tiles_here, 0)
    own_reached = lax.dynamic_slice_in_dim(reached, first_tile, tiles_here, 0)
    slot_ids = jnp.arange(REACH, dtype=jnp.int32)
    cache_stack = jnp.stack([cache_keys, cache_values])

    def query_tile(block_q, tile_index):
        return lax.dynamic_slice_in_dim(block_q, tile_index * TILE, TILE, 0).reshape(
            TILE, heads_here, HD
        )

    def group_blocks(tile_index):
        window = lax.dynamic_slice_in_dim(rim_blocks, tile_index * TILE, 5 * TILE, 1)
        return window.reshape(2, 5, TILE, heads_here, HD)

    widened = with_halo(cache_stack, (("ctx", 1),), cache_keys.shape[0])
    widened = widened.reshape(2, 3 * cache_tiles, TILE, heads_here, HD)

    def one_tile(tile_index):
        local_ids = own_pattern[tile_index] - (ctx_index - 1) * cache_tiles
        picked = jnp.take(widened, local_ids, axis=1)
        blocks = jnp.concatenate([group_blocks(tile_index), picked], axis=1)
        usable_keys = jnp.concatenate([group_valid[tile_index], slot_ids < own_reached[tile_index]])
        return tile_attend(query_tile(local_q, tile_index), blocks[0], blocks[1], usable_keys)

    attended = finish([lax.map(one_tile, jnp.arange(tiles_here, dtype=jnp.int32))])
    gate_part = lax.dynamic_slice_in_dim(gate, lax.axis_index("head") * width, width, 0)
    gated = (attended.reshape(rows, width) * gate_part).astype(jnp.bfloat16)
    return lax.all_to_all(gated, "head", split_axis=0, concat_axis=1, tiled=True)


def solution(mesh):
    placed = (
        P(("ctx", "head"), None),
        P(("ctx", "head"), None),
        P(("ctx", "head"), None),
        P("ctx", "head"),
        P("ctx", "head"),
        P(),
        P(),
        P(),
    )
    return jax.shard_map(
        local, mesh=mesh, in_specs=placed, out_specs=P(("ctx", "head"), None), check_vma=False
    )
```

profile of v0, /device:TPU:18, one launch (start us, length us, event | category | flops | bytes accessed | tf_op | source)
XLA Modules:
  0.0 393.0 jit_solution(12990347110829131353)
XLA Ops:
  0.0 6.2 %pad_maximum_fusion.3 = bf16[2,512,3072]{2,1,0:T(8,128)(2,1)} fusion(bf16[1,512,3072]{2,1,0:T(8,128)(2,1)} %bitcast.120, bf16[1,512,3072]{2,1,0:T(8,128)(2,1)} %bitcast.122), kind=kLoop, calls=%fused_computation.39 | loop fusion | flops 3145728 | bytes 12582912 | tf_op jit(solution)/shard_map/stack | solution.py:74
  6.2 2.0 collective-permute-start.2
  8.2 3.6 collective-permute-start.3
  11.9 1.3 copy.67
  13.2 3.7 all-to-all-start
  16.9 1.3 copy.66
  18.1 18.3 %all-to-all-done = bf16[128,2,3072]{2,0,1:T(8,128)(2,1)S(1)} async-done(((bf16[128,2,3072]{2,0,1:T(8,128)(2,1)}), bf16[128,2,3072]{2,0,1:T(8,128)(2,1)S(1)}, u32[]{:S(2)}, u32[]{:S(2)}) %all-to-all-start) | async-done | bytes 1572896 | tf_op jit(solution)/shard_map/all_to_all | solution.py:55
  36.4 22.5 %all_to_all.67 = bf16[128,2,3072]{2,0,1:T(8,128)(2,1)S(1)} all-to-all(bf16[128,2,3072]{2,0,1:T(8,128)(2,1)} %bitcast.126), channel_id=1, replica_groups=mesh['ctx'=16,'head'=2] {'head'}, dimensions={1} | all-to-all | bytes 3145728 | tf_op jit(solution)/shard_map/all_to_all | solution.py:56
  58.9 2.0 pad_maximum_fusion.4
  60.9 1.9 collective-permute-start
  62.8 3.6 collective-permute-start.1
  66.4 2.6 copy.44
  69.0 4.6 %all-to-all-start.2 = ((bf16[128,2,3072]{0,2,1:T(8,128)(2,1)}), bf16[128,2,3072]{0,2,1:T(8,128)(2,1)}, u32[]{:S(2)}, u32[]{:S(2)}) async-start(bf16[128,2,3072]{0,2,1:T(8,128)(2,1)} %bitcast.125), calls=%async_computation.2 | async-start | bytes 3145728 | tf_op jit(solution)/shard_map/all_to_all | solution.py:54
  73.7 0.1 constant_dynamic-slice_fusion.3
  73.8 0.1 copy.56
  73.9 0.1 dynamic_slice.41
  74.0 0.1 compare_and_fusion.1
  74.0 18.2 %all-to-all-done.2 = bf16[128,2,3072]{0,2,1:T(8,128)(2,1)} async-done(((bf16[128,2,3072]{0,2,1:T(8,128)(2,1)}), bf16[128,2,3072]{0,2,1:T(8,128)(2,1)}, u32[]{:S(2)}, u32[]{:S(2)}) %all-to-all-start.2) | async-done | bytes 1572896 | tf_op jit(solution)/shard_map/all_to_all | solution.py:54
  92.3 2.6 copy.45
  94.8 118.9 %collective-permute-done = bf16[2,256,3072]{2,1,0:T(8,128)(2,1)} collective-permute-done((bf16[2,256,3072]{2,1,0:T(8,128)(2,1)}, bf16[2,256,3072]{2,1,0:T(8,128)(2,1)}, u32[]{:S(2)}, u32[]{:S(2)}) %collective-permute-start) | collective-permute-done | bytes 3145760 | tf_op jit(solution)/shard_map/ppermute | solution.py:19
  213.7 7.9 %pad_maximum_fusion.2 = bf16[2,768,3072]{2,1,0:T(8,128)(2,1)} fusion(bf16[2,256,3072]{2,1,0:T(8,128)(2,1)} %collective-permute-done.1, bf16[1,256,3072]{2,1,0:T(8,128)(2,1)S(1)} %bitcast.119, bf16[1,256,3072]{2,1,0:T(8,128)(2,1)S(1)} %bitcast.117, bf16[2,256,3072]{2,1,0:T(8,128)(2,1)} %collective-permute-done), kind=kLoop, calls=%fused_computation.38 | loop fusion | flops 37748736 | bytes 18874368 | tf_op jit(solution)/shard_map/concatenate | solution.py:23
  221.7 8.4 %pad_maximum_fusion.1 = bf16[2,1536,3072]{2,1,0:T(8,128)(2,1)S(1)} fusion(bf16[2,512,3072]{2,1,0:T(8,128)(2,1)} %collective-permute-done.3, bf16[1,512,3072]{2,1,0:T(8,128)(2,1)S(1)} %bitcast.121, bf16[1,512,3072]{2,1,0:T(8,128)(2,1)S(1)} %bitcast.123, bf16[2,512,3072]{2,1,0:T(8,128)(2,1)} %collective-permute-done.2), kind=kLoop, calls=%fused_computation.37 | loop fusion | flops 75497472 | bytes 37748736 | tf_op jit(solution)/shard_map/concatenate | solution.py:23
  230.0 8.2 %copy.60 = bf16[384,8,24,128]{3,2,1,0:T(8,128)(2,1)} copy(bf16[384,8,24,128]{3,1,2,0:T(8,128)(2,1)S(1)} %bitcast.115) | data formatting | bytes 37748736
  238.3 130.5 %while.17 = (s32[]{:T(128)}, f32[2,128,24,128]{1,3,2,0:T(8,128)}, f32[2,24,128]{2,1,0:T(8,128)S(1)}, f32[2,24,128]{2,1,0:T(8,128)S(1)}, s32[2]{0:T(128)S(1)}, /*...) while((s32[]{:T(128)}, f32[2,128,24,128]{1,3,2,0:T(8,128)}, ...), condition=%wide.region_3.4_spmd.clone, body=%wide.region_0.3_spmd.clone.sunk | while | flops 1861086208 | bytes 177050608 | solution.py:95
  238.3 0.6 dynamic_slice.72
  240.8 10.4 %gather_fusion = bf16[4,2,128,24,128]{4,3,2,1,0:T(8,128)(2,1)} fusion(bf16[2,12,128,24,128]{4,3,2,1,0:T(8,128)(2,1)} %get-tuple-element.348, s32[1024]{0:T(1024)S(1)} %pad_clamp_fusion.2), kind=kCustom, calls=%fused_computation.clone.clone.1 | custom fusion | bytes 12582928 | tf_op jit(solution)/shard_map/while/body/eval_jaxpr/jit(_take)/gather | solution.py:90
  251.2 6.5 %fusion.42 = bf16[2,4,128,24,128]{4,2,1,3,0:T(8,128)(2,1)} fusion(bf16[4,2,128,24,128]{4,3,2,1,0:T(8,128)(2,1)} %gather_fusion, pred[4]{0:T(512)(128)(4,1)S(1)} %compare_and_fusion.3), kind=kLoop, calls=%fused_computation.18.clone.1 | loop fusion | flops 3145728 | bytes 12582916 | tf_op jit(solution)/shard_map/while/body/eval_jaxpr/jit(_take)/select_n | solution.py:90
  258.3 3.9 constant_dynamic-slice_fusion.6
  262.2 5.1 %copy.73 = bf16[160,8,24,128]{3,2,1,0:T(8,128)(2,1)} copy(bf16[160,8,24,128]{3,1,2,0:T(8,128)(2,1)S(1)} %bitcast.110) | data formatting | bytes 15728640 | tf_op jit(solution)/shard_map/while
  267.4 8.5 %copy.74 = bf16[2,5,128,24,128]{4,2,1,3,0:T(8,128)(2,1)} copy(bf16[2,5,128,24,128]{4,3,2,1,0:T(8,128)(2,1)} %bitcast.111) | data formatting | bytes 15728640 | tf_op jit(solution)/shard_map/while/body/eval_jaxpr/reshape | solution.py:83
  275.8 6.6 %pad_maximum_fusion.6 = bf16[1,9,128,24,128]{4,2,1,3,0:T(8,128)(2,1)} fusion(bf16[2,4,128,24,128]{4,2,1,3,0:T(8,128)(2,1)} %fusion.42, bf16[2,5,128,24,128]{4,2,1,3,0:T(8,128)(2,1)} %copy.74), kind=kLoop, calls=%fused_computation.12.clone.1 | loop fusion | flops 3538944 | bytes 21233664 | tf_op jit(solution)/shard_map/while/body/eval_jaxpr/concatenate | solution.py:91
  282.4 1.2 constant_dynamic-slice_fusion.7
  283.6 1.2 copy.75
  284.8 4.4 %fusion.43 = f32[24,128,1152]{1,2,0:S(1)} fusion(bf16[24,128,1152]{1,2,0:T(8,128)(2,1)} %bitcast.112, bf16[128,24,128]{0,2,1:T(8,128)(2,1)} %bitcast.114), kind=kOutput, calls=%fused_computation.52.clone.1 | convolution fusion | flops 905969664 | bytes 22020096 | tf_op jit(solution)/shard_map/while
  289.2 0.6 dynamic_slice.73
  289.8 0.6 iota_compare_fusion.2
  290.5 0.1 pad_add_fusion.2
  290.6 1.9 fusion.44
  292.5 2.9 fusion.45
  295.4 8.1 %bitcast_dynamic-update-slice_fusion.5 = f32[2,128,24,128]{1,3,2,0:T(8,128)} fusion(f32[2,128,24,128]{1,3,2,0:T(8,128)} %get-tuple-element.323, s32[]{:T(128)} %get-tuple-element.322, f32[24,128,9,128]{1,3,2,0:T(8,128)S(1)} %bitcast.109, f32[24,128]{1,0:T(8,128)S(1)} %fusion.44, pred[9]{0:T(512)(128)(4,1)S(1)} %pad_add_fusion.2, ...), kind=kOutput, calls=%fused_computation.19.clone.1 | convolution fusion | flops 923664384 | bytes 29897224 | tf_op jit(solution)/shard_map/while/body/eval_jaxpr/hqnk,nkhd->qhd/dot_general | solution.py:37
  303.5 0.6 dynamic_slice.72
  306.0 10.4 %gather_fusion = bf16[4,2,128,24,128]{4,3,2,1,0:T(8,128)(2,1)} fusion(bf16[2,12,128,24,128]{4,3,2,1,0:T(8,128)(2,1)} %get-tuple-element.348, s32[1024]{0:T(1024)S(1)} %pad_clamp_fusion.2), kind=kCustom, calls=%fused_computation.clone.clone.1 | custom fusion | bytes 12582928 | tf_op jit(solution)/shard_map/while/body/eval_jaxpr/jit(_take)/gather | solution.py:90
  316.4 6.5 %fusion.42 = bf16[2,4,128,24,128]{4,2,1,3,0:T(8,128)(2,1)} fusion(bf16[4,2,128,24,128]{4,3,2,1,0:T(8,128)(2,1)} %gather_fusion, pred[4]{0:T(512)(128)(4,1)S(1)} %compare_and_fusion.3), kind=kLoop, calls=%fused_computation.18.clone.1 | loop fusion | flops 3145728 | bytes 12582916 | tf_op jit(solution)/shard_map/while/body/eval_jaxpr/jit(_take)/select_n | solution.py:90
  323.5 4.0 %constant_dynamic-slice_fusion.6 = bf16[2,640,3072]{2,1,0:T(8,128)(2,1)S(1)} fusion(bf16[2,768,3072]{2,1,0:T(8,128)(2,1)} %get-tuple-element.345, s32[]{:T(128)S(6)} %select_n.103), kind=kLoop, calls=%fused_computation.30.clone.1 | loop fusion | bytes 15728644 | tf_op jit(solution)/shard_map/while/body/eval_jaxpr/dynamic_slice | solution.py:82
  327.5 5.1 %copy.73 = bf16[160,8,24,128]{3,2,1,0:T(8,128)(2,1)} copy(bf16[160,8,24,128]{3,1,2,0:T(8,128)(2,1)S(1)} %bitcast.110) | data formatting | bytes 15728640 | tf_op jit(solution)/shard_map/while
  332.7 8.5 %copy.74 = bf16[2,5,128,24,128]{4,2,1,3,0:T(8,128)(2,1)} copy(bf16[2,5,128,24,128]{4,3,2,1,0:T(8,128)(2,1)} %bitcast.111) | data formatting | bytes 15728640 | tf_op jit(solution)/shard_map/while/body/eval_jaxpr/reshape | solution.py:83
  341.1 6.6 %pad_maximum_fusion.6 = bf16[1,9,128,24,128]{4,2,1,3,0:T(8,128)(2,1)} fusion(bf16[2,4,128,24,128]{4,2,1,3,0:T(8,128)(2,1)} %fusion.42, bf16[2,5,128,24,128]{4,2,1,3,0:T(8,128)(2,1)} %copy.74), kind=kLoop, calls=%fused_computation.12.clone.1 | loop fusion | flops 3538944 | bytes 21233664 | tf_op jit(solution)/shard_map/while/body/eval_jaxpr/concatenate | solution.py:91
  347.7 1.2 constant_dynamic-slice_fusion.7
  348.9 1.2 copy.75
  350.1 4.4 %fusion.43 = f32[24,128,1152]{1,2,0:S(1)} fusion(bf16[24,128,1152]{1,2,0:T(8,128)(2,1)} %bitcast.112, bf16[128,24,128]{0,2,1:T(8,128)(2,1)} %bitcast.114), kind=kOutput, calls=%fused_computation.52.clone.1 | convolution fusion | flops 905969664 | bytes 22020096 | tf_op jit(solution)/shard_map/while
  354.5 0.6 dynamic_slice.73
  355.1 0.6 iota_compare_fusion.2
  355.8 0.1 pad_add_fusion.2
  355.9 1.9 fusion.44
  357.8 2.9 fusion.45
  360.7 8.1 %bitcast_dynamic-update-slice_fusion.5 = f32[2,128,24,128]{1,3,2,0:T(8,128)} fusion(f32[2,128,24,128]{1,3,2,0:T(8,128)} %get-tuple-element.323, s32[]{:T(128)} %get-tuple-element.322, f32[24,128,9,128]{1,3,2,0:T(8,128)S(1)} %bitcast.109, f32[24,128]{1,0:T(8,128)S(1)} %fusion.44, pred[9]{0:T(512)(128)(4,1)S(1)} %pad_add_fusion.2, ...), kind=kOutput, calls=%fused_computation.19.clone.1 | convolution fusion | flops 923664384 | bytes 29897224 | tf_op jit(solution)/shard_map/while/body/eval_jaxpr/hqnk,nkhd->qhd/dot_general | solution.py:37
  368.8 0.0 dynamic-slice-start
  368.8 2.4 multiply_divide_fusion
  371.3 0.0 copy-start.1
  371.3 2.3 copy.54
  373.6 2.2 multiply_convert_fusion
  375.8 14.8 %all_to_all.68 = bf16[2,128,3072]{2,1,0:T(8,128)(2,1)S(1)} all-to-all(bf16[2,128,3072]{2,1,0:T(8,128)(2,1)S(1)} %multiply_convert_fusion), channel_id=1, replica_groups=mesh['ctx'=16,'head'=2] {'head'}, dimensions={0} | all-to-all | bytes 3145728 | tf_op jit(solution)/shard_map/all_to_all | solution.py:98
  390.6 0.9 copy.48
  391.5 1.6 copy.49
  (34 shorter events, 0.2 us)
Async XLA Ops:
  0.0 73.7 %copy-start = (s32[32,4]{0,1:T(4,128)S(1)}, s32[32,4]{0,1:T(4,128)}, u32[]{:S(2)}) copy-start(s32[32,4]{0,1:T(4,128)} %param.15) | copy-start | bytes 1540
  0.0 11.9 %copy-start.4 = (bf16[128,6144]{1,0:T(8,128)(2,1)S(1)}, bf16[128,6144]{1,0:T(8,128)(2,1)}, u32[]{:S(2)}) copy-start(bf16[128,6144]{1,0:T(8,128)(2,1)} %param.11) | copy-start | bytes 4718596
  6.2 10.7 %copy-start.5 = (bf16[128,6144]{1,0:T(8,128)(2,1)S(1)}, bf16[128,6144]{1,0:T(8,128)(2,1)}, u32[]{:S(2)}) copy-start(bf16[128,6144]{1,0:T(8,128)(2,1)} %param.12) | copy-start | bytes 4718596
  6.2 215.5 %collective-permute-start.2 = (bf16[2,512,3072]{2,1,0:T(8,128)(2,1)}, bf16[2,512,3072]{2,1,0:T(8,128)(2,1)}, u32[]{:S(2)}, u32[]{:S(2)}) collective-permute-start(bf16[2,512,3072]{2,1,0:T(8,128)(2,1)} %pad_maximum_fusion.3), channel_id=1, source_target_pairs={{0,2},{2,4},{4,6},{6,8},{8,10},{10,12},{12,14},{14,16},{16,18},{18... | collective-permute-start | bytes 18874376 | tf_op jit(solution)/shard_map/ppermute | solution.py:19
  8.2 213.4 %collective-permute-start.3 = (bf16[2,512,3072]{2,1,0:T(8,128)(2,1)}, bf16[2,512,3072]{2,1,0:T(8,128)(2,1)}, u32[]{:S(2)}, u32[]{:S(2)}) collective-permute-start(bf16[2,512,3072]{2,1,0:T(8,128)(2,1)} %pad_maximum_fusion.3), channel_id=1, source_target_pairs={{2,0},{4,2},{6,4},{8,6},{10,8},{12,10},{14,12},{16,14},{18,16},{20... | collective-permute-start | bytes 18874376 | tf_op jit(solution)/shard_map/ppermute | solution.py:22
  13.2 23.2 %all-to-all-start = ((bf16[128,2,3072]{2,0,1:T(8,128)(2,1)}), bf16[128,2,3072]{2,0,1:T(8,128)(2,1)S(1)}, u32[]{:S(2)}, u32[]{:S(2)}) async-start(bf16[128,2,3072]{2,0,1:T(8,128)(2,1)} %bitcast.72), calls=%async_computation | async-start | bytes 3145728 | tf_op jit(solution)/shard_map/all_to_all | solution.py:55
  58.9 15.0 %copy-start.6 = (s32[32]{0:T(128)S(1)}, s32[32]{0:T(128)}, u32[]{:S(2)}) copy-start(s32[32]{0:T(128)} %param.16) | copy-start | bytes 388
  60.9 152.9 %collective-permute-start = (bf16[2,256,3072]{2,1,0:T(8,128)(2,1)}, bf16[2,256,3072]{2,1,0:T(8,128)(2,1)}, u32[]{:S(2)}, u32[]{:S(2)}) collective-permute-start(bf16[2,256,3072]{2,1,0:T(8,128)(2,1)} %pad_maximum_fusion.4), channel_id=1, source_target_pairs={{0,2},{2,4},{4,6},{6,8},{8,10},{10,12},{12,14},{14,16},{16,18},{18... | collective-permute-start | bytes 9437192 | tf_op jit(solution)/shard_map/ppermute | solution.py:19
  62.8 151.0 %collective-permute-start.1 = (bf16[2,256,3072]{2,1,0:T(8,128)(2,1)}, bf16[2,256,3072]{2,1,0:T(8,128)(2,1)}, u32[]{:S(2)}, u32[]{:S(2)}) collective-permute-start(bf16[2,256,3072]{2,1,0:T(8,128)(2,1)} %pad_maximum_fusion.4), channel_id=1, source_target_pairs={{2,0},{4,2},{6,4},{8,6},{10,8},{12,10},{14,12},{16,14},{18,16},{20... | collective-permute-start | bytes 9437192 | tf_op jit(solution)/shard_map/ppermute | solution.py:22
  69.0 23.3 %all-to-all-start.2 = ((bf16[128,2,3072]{0,2,1:T(8,128)(2,1)}), bf16[128,2,3072]{0,2,1:T(8,128)(2,1)}, u32[]{:S(2)}, u32[]{:S(2)}) async-start(bf16[128,2,3072]{0,2,1:T(8,128)(2,1)} %bitcast.125), calls=%async_computation.2 | async-start | bytes 3145728 | tf_op jit(solution)/shard_map/all_to_all | solution.py:54
  94.8 126.8 %copy-start.2 = (bf16[512,3072]{1,0:T(8,128)(2,1)S(1)}, bf16[512,3072]{1,0:T(8,128)(2,1)}, u32[]{:S(2)}) copy-start(bf16[512,3072]{1,0:T(8,128)(2,1)} %param.14) | copy-start | bytes 9437188
  94.8 126.8 %copy-start.3 = (bf16[512,3072]{1,0:T(8,128)(2,1)S(1)}, bf16[512,3072]{1,0:T(8,128)(2,1)}, u32[]{:S(2)}) copy-start(bf16[512,3072]{1,0:T(8,128)(2,1)} %param.13) | copy-start | bytes 9437188
  368.8 4.8 %dynamic-slice-start = ((f32[6144]{0:T(1024)}, s32[]{:T(128)}), f32[3072]{0:T(1024)S(1)}, s32[]{:S(2)}) async-start(f32[6144]{0:T(1024)} %param.17, s32[]{:T(128)} %select_n.57), calls=%async_computation.4 | async-start | bytes 25088 | tf_op jit(solution)/shard_map/dynamic_slice | solution.py:96
  371.3 21.8 %copy-start.1 = (s32[32,4]{0,1:T(4,128)S(1)}, s32[32,4]{0,1:T(4,128)}, u32[]{:S(2)}) copy-start(s32[32,4]{0,1:T(4,128)} %param.15) | copy-start | bytes 1540
where the time goes:
time: 394 us; the launch traced here: 393 us
  waiting for transfers between devices  155 us (39%)
  local copies, waits for them, and re-layouts  84.1 us (21%)
  other arithmetic  66.3 us (17%)
  blocking collectives  37.3 us (9%)
  matrix products  25 us (6%)
  starting transfers between devices  19.6 us (5%)
  loops' own time  5.2 us (1%)
    ppermute x2, waiting for transfers between devices, with_halo(): lax.ppermute(lax.slice_in_dim(block, block.shape[dim] - width, None, axis...  119 us
    all_to_all x1, blocking collectives, local(): lax.all_to_all(values, 'head', split_axis=1, concat_axis=0, tiled=True)  22.5 us
    gather x2, local copies, waits for them, and re-layouts, one_tile(): picked = jnp.take(widened, local_ids, axis=1)  20.7 us
    all_to_all x1, waiting for transfers between devices, local(): lax.all_to_all(keys, 'head', split_axis=1, concat_axis=0, tiled=True)  18.3 us
    all_to_all x1, waiting for transfers between devices, local(): lax.all_to_all(queries, 'head', split_axis=1, concat_axis=0, tiled=True)  18.2 us
    reshape x2, local copies, waits for them, and re-layouts, group_blocks(): return window.reshape(2, 5, TILE, heads_here, HD)  16.9 us
    concatenate x2, other arithmetic, with_halo(): block = jnp.concatenate([low, block, high], axis=dim)  16.3 us
    dot_general x2, matrix products, tile_attend(): jnp.einsum('hqnk,nkhd->qhd', weights, value_blocks, preferred_element_typ...  16.1 us
  transfers between devices with their start and end apart: 6, of which 3 were waited for; matrix products, arithmetic and copies ran while one was open for 5% of the time, Pallas kernels for 0%

commit v1 on v0

v1 whole, which is shorter than its diff:
```python
import functools
import math

import jax
import jax.numpy as jnp
from jax import lax
from jax.experimental import pallas as pl
from jax.experimental.pallas import tpu as pltpu
from jax.sharding import PartitionSpec as P

HD = 128
TILE = 128
REACH = 4
NEGATIVE = -1e30
LOG2E = math.log2(math.e)
GROUP = 2
AHEAD = 3
NT = (((1,), (1,)), ((), ()))
NN = (((1,), (0,)), ((), ()))


def kernel(sizes, q_ref, k_ref, v_ref, ck_ref, cv_ref, pattern_ref, reached_ref, gate_ref, out_ref,
           qs, ks, vs, cks, cvs, qn, po, pi, lo, li, oacc, macc, lacc, ob, bias,
           loc_sem, y_ssem, y_rsem, n_ssem, n_rsem, p_ssem, p_rsem, l_ssem, l_rsem, o_ssem, o_rsem, oloc_sem):
    n_ctx, n_head, rows, width, cw, hc, nch, tiles_here, cache_tiles = sizes
    c = lax.axis_index("ctx")
    h = lax.axis_index("head")
    has = (c > 0, c < n_ctx - 1)
    side_id = (c - 1, c + 1)
    all_rows = n_head * rows

    def at_head(d):
        return lax.rem(h + d, n_head)

    def from_head(d):
        return lax.rem(h - d + n_head, n_head)

    def row_block(i):
        return pl.ds(pl.multiple_of(i * rows, rows), rows)

    def columns(i, j):
        return pl.ds(pl.multiple_of(i * width + j * cw, cw), cw)

    def local_in(j):
        mine = row_block(h)
        pairs = [
            (q_ref.at[:, columns(h, j)], qs.at[j, mine, :]),
            (k_ref.at[:, columns(h, j)], ks.at[j, mine, :]),
            (v_ref.at[:, columns(h, j)], vs.at[j, mine, :]),
            (ck_ref.at[:, columns(0, j)], cks.at[j]),
            (cv_ref.at[:, columns(0, j)], cvs.at[j]),
        ]
        return [pltpu.make_async_copy(s, t, loc_sem.at[n, j]) for n, (s, t) in enumerate(pairs)]

    def exchange(t, d, j):
        src = (q_ref, k_ref, v_ref)[t]
        dst = (qs, ks, vs)[t]
        to = at_head(d)
        return pltpu.make_async_remote_copy(
            src_ref=src.at[:, columns(to, j)], dst_ref=dst.at[j, row_block(h), :],
            send_sem=y_ssem.at[t, d - 1, j], recv_sem=y_rsem.at[t, d - 1, j],
            device_id=(c, to), device_id_type=pl.DeviceIdType.MESH)

    def exchange_in(t, d, j):
        dst = (qs, ks, vs)[t].at[j, row_block(from_head(d)), :]
        return pltpu.make_async_remote_copy(
            src_ref=dst, dst_ref=dst,
            send_sem=y_ssem.at[t, d - 1, j], recv_sem=y_rsem.at[t, d - 1, j],
            device_id=(c, from_head(d)), device_id_type=pl.DeviceIdType.MESH)

    def query_out(s, d, j):
        piece = row_block(from_head(d))
        src = q_ref.at[:, columns(h, j)] if d == 0 else qs.at[j, piece, :]
        return pltpu.make_async_remote_copy(
            src_ref=src, dst_ref=qn.at[1 - s, j, piece, :],
            send_sem=n_ssem.at[s, d, j], recv_sem=n_rsem.at[1 - s, d, j],
            device_id=(side_id[s], h), device_id_type=pl.DeviceIdType.MESH)

    def query_in(s, d, j):
        dst = qn.at[s, j, row_block(from_head(d)), :]
        return pltpu.make_async_remote_copy(
            src_ref=dst, dst_ref=dst,
            send_sem=n_ssem.at[s, d, j], recv_sem=n_rsem.at[s, d, j],
            device_id=(side_id[s], h), device_id_type=pl.DeviceIdType.MESH)

    def part_out(s, j):
        return [
            pltpu.make_async_remote_copy(
                src_ref=src.at[s, j], dst_ref=dst.at[1 - s, j],
                send_sem=ss.at[s, j], recv_sem=rs.at[1 - s, j],
                device_id=(side_id[s], h), device_id_type=pl.DeviceIdType.MESH)
            for src, dst, ss, rs in ((po, pi, p_ssem, p_rsem), (lo, li, l_ssem, l_rsem))
        ]

    def part_in(s, j):
        return [
            pltpu.make_async_remote_copy(
                src_ref=dst.at[s, j], dst_ref=dst.at[s, j],
                send_sem=ss.at[s, j], recv_sem=rs.at[s, j],
                device_id=(side_id[s], h), device_id_type=pl.DeviceIdType.MESH)
            for dst, ss, rs in ((pi, p_ssem, p_rsem), (li, l_ssem, l_rsem))
        ]

    def result_out(d, j):
        to = at_head(d)
        return pltpu.make_async_remote_copy(
            src_ref=ob.at[j, row_block(to), :], dst_ref=out_ref.at[:, columns(h, j)],
            send_sem=o_ssem.at[d - 1, j], recv_sem=o_rsem.at[d - 1, j],
            device_id=(c, to), device_id_type=pl.DeviceIdType.MESH)

    def result_in(d, j):
        dst = out_ref.at[:, columns(from_head(d), j)]
        return pltpu.make_async_remote_copy(
            src_ref=dst, dst_ref=dst,
            send_sem=o_ssem.at[d - 1, j], recv_sem=o_rsem.at[d - 1, j],
            device_id=(c, from_head(d)), device_id_type=pl.DeviceIdType.MESH)

    def result_local(j):
        return pltpu.make_async_copy(
            ob.at[j, row_block(h), :], out_ref.at[:, columns(h, j)], oloc_sem.at[j])

    barrier = pltpu.get_barrier_semaphore()
    for d in range(1, n_head):
        pl.semaphore_signal(barrier, inc=1, device_id=(c, at_head(d)), device_id_type=pl.DeviceIdType.MESH)
    for s in range(2):
        @pl.when(has[s])
        def _():
            pl.semaphore_signal(barrier, inc=1, device_id=(side_id[s], h), device_id_type=pl.DeviceIdType.MESH)

    @pl.loop(0, nch)
    def _(j):
        for copy in local_in(j):
            copy.start()

    for s in range(3):
        source = jnp.clip(c + (-1, 1, 0)[s], 0, n_ctx - 1)
        for t in range(tiles_here):
            g = source * tiles_here + t
            used = reached_ref[g]
            for b in range(tiles_here):
                away = g - (c * tiles_here + b)
                near = jnp.where((away >= -2) & (away <= 2), 0.0, NEGATIVE)
                bias[s, pl.ds(b, 1), pl.ds(t * TILE, TILE)] = jnp.full((1, TILE), near, jnp.float32)
            for b in range(cache_tiles):
                times = jnp.int32(0)
                for r in range(REACH):
                    hit = (pattern_ref[g, r] == c * cache_tiles + b) & (r < used)
                    times = times + jnp.where(hit, 1, 0)
                log = jnp.float32(NEGATIVE)
                for n in range(1, REACH + 1):
                    log = jnp.where(times == n, jnp.float32(math.log2(n)), log)
                bias[s, pl.ds(tiles_here + b, 1), pl.ds(t * TILE, TILE)] = jnp.full((1, TILE), log, jnp.float32)

    peers = n_head - 1 + jnp.where(has[0], 1, 0) + jnp.where(has[1], 1, 0)
    pl.semaphore_wait(barrier, peers)

    def send_chunk(j):
        for t in range(3):
            for d in range(1, n_head):
                exchange(t, d, j).start()
        for s in range(2):
            @pl.when(has[s])
            def _():
                query_out(s, 0, j).start()

    ahead = min(AHEAD, nch)

    @pl.loop(0, ahead)
    def _(j):
        send_chunk(j)

    scale = HD ** -0.5 * LOG2E

    def partial(s, q, k_block, k_cache, v_turned):
        near = lax.dot_general(k_block, q, NT, preferred_element_type=jnp.float32)
        far = lax.dot_general(k_cache, q, NT, preferred_element_type=jnp.float32)
        parts = []
        for b in range(tiles_here + cache_tiles):
            block = near[b * TILE:(b + 1) * TILE] if b < tiles_here else (
                far[(b - tiles_here) * TILE:(b - tiles_here + 1) * TILE])
            parts.append(block * scale + bias[s, pl.ds(b, 1), :])
        scores = jnp.concatenate(parts, axis=0)
        peak = jnp.max(scores, axis=0, keepdims=True)
        expos = jnp.exp2(scores - peak)
        total = jnp.sum(expos, axis=0, keepdims=True)
        summed = lax.dot_general(v_turned, expos.astype(jnp.bfloat16), NN, preferred_element_type=jnp.float32)
        return summed, peak, total

    def relay(j):
        for d in range(1, n_head):
            exchange_in(0, d, j).wait_recv()
            for s in range(2):
                @pl.when(has[s])
                def _():
                    query_out(s, d, j).start()

    def attend(j):
        for copy in local_in(j):
            copy.wait()
        for t in (1, 2):
            for d in range(1, n_head):
                exchange_in(t, d, j).wait_recv()
        for s in range(2):
            @pl.when(has[s])
            def _():
                for d in range(n_head):
                    query_in(s, d, j).wait_recv()
        for i in range(hc):
            cols = slice(i * HD, (i + 1) * HD)
            k_block, k_cache = ks[j, :, cols], cks[j, :, cols]
            v_turned = jnp.concatenate([vs[j, :, cols].T, cvs[j, :, cols].T], axis=1)
            for s in range(2):
                @pl.when(has[s])
                def _():
                    summed, peak, total = partial(s, qn[s, j, :, cols], k_block, k_cache, v_turned)
                    po[s, j, i] = (summed * (1.0 / total)).astype(jnp.bfloat16)
                    lo[s, j, pl.ds(i, 1), :] = peak + jnp.log2(total)
            summed, peak, total = partial(2, qs[j, :, cols], k_block, k_cache, v_turned)
            oacc[j, i] = summed
            macc[j, pl.ds(i, 1), :] = peak
            lacc[j, pl.ds(i, 1), :] = total
        for s in range(2):
            @pl.when(has[s])
            def _():
                for copy in part_out(s, j):
                    copy.start()

    def combine(j):
        for s in range(2):
            @pl.when(has[s])
            def _():
                for copy in part_in(s, j):
                    copy.wait_recv()

            @pl.when(jnp.logical_not(has[s]))
            def _():
                pi[s, j] = jnp.zeros(pi.shape[2:], pi.dtype)
                li[s, j] = jnp.full(li.shape[2:], NEGATIVE, li.dtype)
        for i in range(hc):
            m_own, m_low, m_high = macc[j, pl.ds(i, 1), :], li[0, j, pl.ds(i, 1), :], li[1, j, pl.ds(i, 1), :]
            top = jnp.maximum(m_own, jnp.maximum(m_low, m_high))
            f_own, f_low, f_high = jnp.exp2(m_own - top), jnp.exp2(m_low - top), jnp.exp2(m_high - top)
            inverse = 1.0 / (f_own * lacc[j, pl.ds(i, 1), :] + f_low + f_high)
            mixed = (oacc[j, i] * (f_own * inverse) + pi[0, j, i].astype(jnp.float32) * (f_low * inverse)
                     + pi[1, j, i].astype(jnp.float32) * (f_high * inverse))
            gain = gate_ref[pl.ds(h * (width // HD) + j * hc + i, 1), :]
            ob[j, :, i * HD:(i + 1) * HD] = (mixed.T * gain).astype(jnp.bfloat16)
        for d in range(1, n_head):
            result_out(d, j).start()
        result_local(j).start()

    @pl.loop(0, nch + 2)
    def _(i):
        @pl.when(i + ahead < nch)
        def _():
            send_chunk(i + ahead)

        @pl.when(i < nch)
        def _():
            relay(i)

        @pl.when((i >= 1) & (i <= nch))
        def _():
            attend(i - 1)

        @pl.when(i >= 2)
        def _():
            combine(i - 2)

    @pl.loop(0, nch)
    def _(j):
        for t in range(3):
            for d in range(1, n_head):
                exchange(t, d, j).wait_send()
        for s in range(2):
            @pl.when(has[s])
            def _():
                for d in range(n_head):
                    query_out(s, d, j).wait_send()
                for copy in part_out(s, j):
                    copy.wait_send()
        for d in range(1, n_head):
            result_out(d, j).wait_send()
            result_in(d, j).wait_recv()
        result_local(j).wait()


def local(n_ctx, n_head, queries, keys, values, cache_keys, cache_values, pattern, reached, gate):
    rows, model = queries.shape
    width = cache_keys.shape[1]
    heads_here = width // HD
    hc = max(n for n in range(1, GROUP + 1) if heads_here % n == 0)
    cw = hc * HD
    nch = heads_here // hc
    all_rows = rows * n_head
    tiles_here = all_rows // TILE
    cache_rows = cache_keys.shape[0]
    cache_tiles = cache_rows // TILE
    sizes = (n_ctx, n_head, rows, width, cw, hc, nch, tiles_here, cache_tiles)
    bf, f32 = jnp.bfloat16, jnp.float32
    dma = pltpu.SemaphoreType.DMA
    hbm = pl.BlockSpec(memory_space=pl.ANY)
    smem = pl.BlockSpec(memory_space=pltpu.SMEM)
    own = max(n_head - 1, 1)
    return pl.pallas_call(
        functools.partial(kernel, sizes),
        out_shape=jax.ShapeDtypeStruct((rows, model), bf),
        in_specs=[hbm] * 5 + [smem, smem, pl.BlockSpec(memory_space=pltpu.VMEM)],
        out_specs=hbm,
        scratch_shapes=[
            pltpu.VMEM((nch, all_rows, cw), bf),
            pltpu.VMEM((nch, all_rows, cw), bf),
            pltpu.VMEM((nch, all_rows, cw), bf),
            pltpu.VMEM((nch, cache_rows, cw), bf),
            pltpu.VMEM((nch, cache_rows, cw), bf),
            pltpu.VMEM((2, nch, all_rows, cw), bf),
            pltpu.VMEM((2, nch, hc, HD, all_rows), bf),
            pltpu.VMEM((2, nch, hc, HD, all_rows), bf),
            pltpu.VMEM((2, nch, 8, all_rows), f32),
            pltpu.VMEM((2, nch, 8, all_rows), f32),
            pltpu.VMEM((nch, hc, HD, all_rows), f32),
            pltpu.VMEM((nch, 8, all_rows), f32),
            pltpu.VMEM((nch, 8, all_rows), f32),
            pltpu.VMEM((nch, all_rows, cw), bf),
            pltpu.VMEM((3, -(-(tiles_here + cache_tiles) // 8) * 8, all_rows), f32),
            dma((5, nch)),
            dma((3, own, nch)), dma((3, own, nch)),
            dma((2, n_head, nch)), dma((2, n_head, nch)),
            dma((2, nch)), dma((2, nch)),
            dma((2, nch)), dma((2, nch)),
            dma((own, nch)), dma((own, nch)),
            dma((nch,)),
        ],
        compiler_params=pltpu.CompilerParams(
            collective_id=0, has_side_effects=True, vmem_limit_bytes=56 * 1024 * 1024),
    )(queries, keys, values, cache_keys, cache_values, pattern, reached, gate.reshape(model // HD, HD))


def solution(mesh):
    placed = (
        P(("ctx", "head"), None),
        P(("ctx", "head"), None),
        P(("ctx", "head"), None),
        P("ctx", "head"),
        P("ctx", "head"),
        P(),
        P(),
        P(),
    )
    return jax.shard_map(
        functools.partial(local, mesh.shape["ctx"], mesh.shape["head"]),
        mesh=mesh, in_specs=placed, out_specs=P(("ctx", "head"), None), check_vma=False
    )
```

time: 394 us -> 96.8 us (0.25)
  waiting for transfers between devices: 155 us -> 0 us
  Pallas kernels: 0 us -> 92.4 us
  local copies, waits for them, and re-layouts: 84.1 us -> 4.06 us
  other arithmetic: 66.3 us -> 0 us
  blocking collectives: 37.3 us -> 0 us
  matrix products: 25 us -> 0 us
  starting transfers between devices: 19.6 us -> 0 us
  loops' own time: 5.2 us -> 0 us
    ppermute x4 -> x0, waiting for transfers between devices: 119 us -> none  [the longest x2 119 us: with_halo(): lax.ppermute(lax.slice_in_dim(block, block.shape[dim] - width, None, axis...]
    pallas_call x0 -> x1, Pallas kernels: none -> 92.4 us  [local(): pl.pallas_call(functools.partial(kernel, sizes), out_shape=jax.ShapeDtype...]
    all_to_all x2 -> x0, blocking collectives: 37.3 us -> none  [the longest x1 22.5 us: local(): lax.all_to_all(values, 'head', split_axis=1, concat_axis=0, tiled=True)]
    all_to_all x2 -> x0, waiting for transfers between devices: 36.5 us -> none  [the longest x1 18.3 us: local(): lax.all_to_all(keys, 'head', split_axis=1, concat_axis=0, tiled=True)]
    concatenate x6 -> x0, other arithmetic: 29.6 us -> none  [the longest x2 16.3 us: with_halo(): block = jnp.concatenate([low, block, high], axis=dim)]
    gather x2 -> x0, local copies, waits for them, and re-layouts: 20.7 us -> none  [one_tile(): picked = jnp.take(widened, local_ids, axis=1)]
    reshape x3 -> x0, local copies, waits for them, and re-layouts: 19.3 us -> none  [the longest x2 16.9 us: group_blocks(): return window.reshape(2, 5, TILE, heads_here, HD)]
    dot_general x2 -> x0, matrix products: 16.1 us -> none  [tile_attend(): jnp.einsum('hqnk,nkhd->qhd', weights, value_blocks, preferred_element_typ...]
  transfers between devices with their start and end apart: 6 -> 0, of which waited for: 3 -> 0; matrix products, arithmetic and copies ran while one was open for 5% -> 0% of each run, Pallas kernels for 0% -> 0%
where the time goes in v1:
time: 96.8 us; the launch traced here: 96.5 us
  Pallas kernels  92.4 us (95%)
  local copies, waits for them, and re-layouts  4.06 us (4%)
    pallas_call x1, Pallas kernels, local(): pl.pallas_call(functools.partial(kernel, sizes), out_shape=jax.ShapeDtype...  92.4 us
    unnamed x2, local copies, waits for them, and re-layouts  4.06 us

profile of v1, /device:TPU:18, one launch (start us, length us, event | category | flops | bytes accessed | tf_op | source)
XLA Modules:
  0.0 96.5 jit_solution(10150443533378004107)
XLA Ops:
  0.0 1.4 %copy.9.pattern_ref = s32[32,4]{1,0:T(8,128)} copy(s32[32,4]{0,1:T(4,128)} %param.13) | data formatting | bytes 1024 | tf_op args[5]
  1.4 92.4 %shard_map.82 = bf16[128,6144]{1,0:T(8,128)(2,1)} custom-call(bf16[128,6144]{1,0:T(8,128)(2,1)} %q_ref.1, bf16[128,6144]{1,0:T(8,128)(2,1)} %k_ref.1, bf16[128,6144]{1,0:T(8,128)(2,1)} %v_ref.1, bf16[512,3072]{1,0:T(8,128)(2,1)} %ck_ref.1, bf16[512,3072]{1,0:T(8,128)(2,1)} %cv_ref.1, s32[32,4]{1,0:T(8,128)} %copy.9.pattern_ref, s32[32]{0:T(128)} %reached_ref.1, ...), custom_call_target="tpu_custom_call" | custom-call | tf_op jit(solution)/shard_map/pallas_call | solution.py:305
  93.8 2.7 %copy.11 = bf16[128,6144]{1,0:T(8,128)(2,1)} copy(bf16[128,6144]{1,0:T(8,128)(2,1)} %shard_map.82) | data formatting | bytes 3145728

commit v2 on v1

--- a/solution.py
+++ b/solution.py
@@ -13,7 +13,7 @@
 REACH = 4
 NEGATIVE = -1e30
 LOG2E = math.log2(math.e)
-GROUP = 2
+GROUP = 4
 AHEAD = 3
 NT = (((1,), (1,)), ((), ()))
 NN = (((1,), (0,)), ((), ()))
@@ -154,6 +154,15 @@
     peers = n_head - 1 + jnp.where(has[0], 1, 0) + jnp.where(has[1], 1, 0)
     pl.semaphore_wait(barrier, peers)
 
+    for s in range(2):
+        @pl.when(jnp.logical_not(has[s]))
+        def _():
+            @pl.loop(0, nch)
+            def _(j):
+                qn[s, j] = jnp.zeros(qn.shape[2:], qn.dtype)
+                pi[s, j] = jnp.zeros(pi.shape[2:], pi.dtype)
+                li[s, j] = jnp.full(li.shape[2:], NEGATIVE, li.dtype)
+
     def send_chunk(j):
         for t in range(3):
             for d in range(1, n_head):
@@ -171,20 +180,23 @@
 
     scale = HD ** -0.5 * LOG2E
 
-    def partial(s, q, k_block, k_cache, v_turned):
-        near = lax.dot_general(k_block, q, NT, preferred_element_type=jnp.float32)
-        far = lax.dot_general(k_cache, q, NT, preferred_element_type=jnp.float32)
-        parts = []
+    def partial(s, near, far):
+        blocks, gains, peak = [], [], None
         for b in range(tiles_here + cache_tiles):
             block = near[b * TILE:(b + 1) * TILE] if b < tiles_here else (
                 far[(b - tiles_here) * TILE:(b - tiles_here + 1) * TILE])
-            parts.append(block * scale + bias[s, pl.ds(b, 1), :])
-        scores = jnp.concatenate(parts, axis=0)
-        peak = jnp.max(scores, axis=0, keepdims=True)
-        expos = jnp.exp2(scores - peak)
-        total = jnp.sum(expos, axis=0, keepdims=True)
-        summed = lax.dot_general(v_turned, expos.astype(jnp.bfloat16), NN, preferred_element_type=jnp.float32)
-        return summed, peak, total
+            gain = bias[s, pl.ds(b, 1), :]
+            tall = jnp.max(block, axis=0, keepdims=True) * scale + gain
+            peak = tall if peak is None else jnp.maximum(peak, tall)
+            blocks.append(block)
+            gains.append(gain)
+        total, weights = 0.0, []
+        for block, gain in zip(blocks, gains):
+            expos = jnp.exp2(block * scale + (gain - peak))
+            total = total + jnp.sum(expos, axis=0, keepdims=True)
+            weights.append(expos.astype(jnp.bfloat16))
+        weights = jnp.concatenate(weights, axis=0)
+        return weights, peak, total
 
     def relay(j):
         for d in range(1, n_head):
@@ -205,20 +217,38 @@
             def _():
                 for d in range(n_head):
                     query_in(s, d, j).wait_recv()
-        for i in range(hc):
+        units = [(i, s) for i in range(hc) for s in range(3)]
+        turned, raw, soft = {}, {}, {}
+
+        def score(i, s):
             cols = slice(i * HD, (i + 1) * HD)
-            k_block, k_cache = ks[j, :, cols], cks[j, :, cols]
-            v_turned = jnp.concatenate([vs[j, :, cols].T, cvs[j, :, cols].T], axis=1)
-            for s in range(2):
-                @pl.when(has[s])
-                def _():
-                    summed, peak, total = partial(s, qn[s, j, :, cols], k_block, k_cache, v_turned)
-                    po[s, j, i] = (summed * (1.0 / total)).astype(jnp.bfloat16)
-                    lo[s, j, pl.ds(i, 1), :] = peak + jnp.log2(total)
-            summed, peak, total = partial(2, qs[j, :, cols], k_block, k_cache, v_turned)
-            oacc[j, i] = summed
-            macc[j, pl.ds(i, 1), :] = peak
-            lacc[j, pl.ds(i, 1), :] = total
+            if s == 0:
+                turned[i] = jnp.concatenate([vs[j, :, cols].T, cvs[j, :, cols].T], axis=1)
+            q = qs[j, :, cols] if s == 2 else qn[s, j, :, cols]
+            raw[i, s] = (lax.dot_general(ks[j, :, cols], q, NT, preferred_element_type=jnp.float32),
+                         lax.dot_general(cks[j, :, cols], q, NT, preferred_element_type=jnp.float32))
+
+        def weigh(i, s):
+            soft[i, s] = partial(s, *raw.pop((i, s)))
+
+        def gather(i, s):
+            weights, peak, total = soft.pop((i, s))
+            summed = lax.dot_general(turned[i], weights, NN, preferred_element_type=jnp.float32)
+            if s < 2:
+                po[s, j, i] = (summed * (1.0 / total)).astype(jnp.bfloat16)
+                lo[s, j, pl.ds(i, 1), :] = peak + jnp.log2(total)
+            else:
+                oacc[j, i] = summed
+                macc[j, pl.ds(i, 1), :] = peak
+                lacc[j, pl.ds(i, 1), :] = total
+
+        for n in range(len(units) + 2):
+            if n < len(units):
+                score(*units[n])
+            if n >= 2:
+                gather(*units[n - 2])
+            if 1 <= n <= len(units):
+                weigh(*units[n - 1])
         for s in range(2):
             @pl.when(has[s])
             def _():
@@ -231,11 +261,6 @@
             def _():
                 for copy in part_in(s, j):
                     copy.wait_recv()
-
-            @pl.when(jnp.logical_not(has[s]))
-            def _():
-                pi[s, j] = jnp.zeros(pi.shape[2:], pi.dtype)
-                li[s, j] = jnp.full(li.shape[2:], NEGATIVE, li.dtype)
         for i in range(hc):
             m_own, m_low, m_high = macc[j, pl.ds(i, 1), :], li[0, j, pl.ds(i, 1), :], li[1, j, pl.ds(i, 1), :]
             top = jnp.maximum(m_own, jnp.maximum(m_low, m_high))

time: 96.8 us -> 87.2 us (0.901)
  Pallas kernels: 92.4 us -> 82.5 us
    pallas_call x1, Pallas kernels: 92.4 us -> 82.5 us  [local(): pl.pallas_call(functools.partial(kernel, sizes), out_shape=jax.ShapeDtype...]
where the time goes in v2:
time: 87.2 us; the launch traced here: 86.5 us
  Pallas kernels  82.5 us (95%)
  local copies, waits for them, and re-layouts  4.06 us (5%)
    pallas_call x1, Pallas kernels, local(): pl.pallas_call(functools.partial(kernel, sizes), out_shape=jax.ShapeDtype...  82.5 us
    unnamed x2, local copies, waits for them, and re-layouts  4.06 us

profile of v2, /device:TPU:18, one launch (start us, length us, event | category | flops | bytes accessed | tf_op | source)
XLA Modules:
  0.0 86.5 jit_solution(15823455426699549607)
XLA Ops:
  0.0 1.4 %copy.9.pattern_ref = s32[32,4]{1,0:T(8,128)} copy(s32[32,4]{0,1:T(4,128)} %param.13) | data formatting | bytes 1024 | tf_op args[5]
  1.4 82.5 %shard_map.82 = bf16[128,6144]{1,0:T(8,128)(2,1)} custom-call(bf16[128,6144]{1,0:T(8,128)(2,1)} %q_ref.1, bf16[128,6144]{1,0:T(8,128)(2,1)} %k_ref.1, bf16[128,6144]{1,0:T(8,128)(2,1)} %v_ref.1, bf16[512,3072]{1,0:T(8,128)(2,1)} %ck_ref.1, bf16[512,3072]{1,0:T(8,128)(2,1)} %cv_ref.1, s32[32,4]{1,0:T(8,128)} %copy.9.pattern_ref, s32[32]{0:T(128)} %reached_ref.1, ...), custom_call_target="tpu_custom_call" | custom-call | tf_op jit(solution)/shard_map/pallas_call | solution.py:330
  83.8 2.7 %copy.11 = bf16[128,6144]{1,0:T(8,128)(2,1)} copy(bf16[128,6144]{1,0:T(8,128)(2,1)} %shard_map.82) | data formatting | bytes 3145728

commit v3 on v2

--- a/solution.py
+++ b/solution.py
@@ -15,6 +15,7 @@
 LOG2E = math.log2(math.e)
 GROUP = 4
 AHEAD = 3
+LEAD = 1
 NT = (((1,), (1,)), ((), ()))
 NN = (((1,), (0,)), ((), ()))
 
@@ -163,16 +164,29 @@
                 pi[s, j] = jnp.zeros(pi.shape[2:], pi.dtype)
                 li[s, j] = jnp.full(li.shape[2:], NEGATIVE, li.dtype)
 
+    def send_queries(j):
+        for d in range(1, n_head):
+            exchange(0, d, j).start()
+        for s in range(2):
+            @pl.when(has[s])
+            def _():
+                query_out(s, 0, j).start()
+
     def send_chunk(j):
-        for t in range(3):
+        @pl.when(j + lead < nch)
+        def _():
+            send_queries(j + lead)
+
+        for u in (1, 2):
             for d in range(1, n_head):
-                exchange(t, d, j).start()
-        for s in range(2):
-            @pl.when(has[s])
-            def _():
-                query_out(s, 0, j).start()
+                exchange(u, d, j).start()
 
     ahead = min(AHEAD, nch)
+    lead = min(LEAD, nch)
+
+    @pl.loop(0, lead)
+    def _(j):
+        send_queries(j)
 
     @pl.loop(0, ahead)
     def _(j):
@@ -217,7 +231,6 @@
             def _():
                 for d in range(n_head):
                     query_in(s, d, j).wait_recv()
-        units = [(i, s) for i in range(hc) for s in range(3)]
         turned, raw, soft = {}, {}, {}
 
         def score(i, s):
@@ -242,18 +255,22 @@
                 macc[j, pl.ds(i, 1), :] = peak
                 lacc[j, pl.ds(i, 1), :] = total
 
-        for n in range(len(units) + 2):
-            if n < len(units):
-                score(*units[n])
-            if n >= 2:
-                gather(*units[n - 2])
-            if 1 <= n <= len(units):
-                weigh(*units[n - 1])
+        def run(units):
+            for n in range(len(units) + 2):
+                if n < len(units):
+                    score(*units[n])
+                if n >= 2:
+                    gather(*units[n - 2])
+                if 1 <= n <= len(units):
+                    weigh(*units[n - 1])
+
+        run([(i, s) for i in range(hc) for s in range(2)])
         for s in range(2):
             @pl.when(has[s])
             def _():
                 for copy in part_out(s, j):
                     copy.start()
+        run([(i, 2) for i in range(hc)])
 
     def combine(j):
         for s in range(2):

time: 87.2 us -> 85 us (0.975)
  Pallas kernels: 82.5 us -> 80.7 us
    pallas_call x1, Pallas kernels: 82.5 us -> 80.7 us  [local(): pl.pallas_call(functools.partial(kernel, sizes), out_shape=jax.ShapeDtype...]
where the time goes in v3:
time: 85 us; the launch traced here: 84.8 us
  Pallas kernels  80.7 us (95%)
  local copies, waits for them, and re-layouts  4.06 us (5%)
    pallas_call x1, Pallas kernels, local(): pl.pallas_call(functools.partial(kernel, sizes), out_shape=jax.ShapeDtype...  80.7 us
    unnamed x2, local copies, waits for them, and re-layouts  4.06 us

profile of v3, /device:TPU:18, one launch (start us, length us, event | category | flops | bytes accessed | tf_op | source)
XLA Modules:
  0.0 84.8 jit_solution(12121655401022313918)
XLA Ops:
  0.0 1.4 %copy.9.pattern_ref = s32[32,4]{1,0:T(8,128)} copy(s32[32,4]{0,1:T(4,128)} %param.13) | data formatting | bytes 1024 | tf_op args[5]
  1.4 80.7 %shard_map.82 = bf16[128,6144]{1,0:T(8,128)(2,1)} custom-call(bf16[128,6144]{1,0:T(8,128)(2,1)} %q_ref.1, bf16[128,6144]{1,0:T(8,128)(2,1)} %k_ref.1, bf16[128,6144]{1,0:T(8,128)(2,1)} %v_ref.1, bf16[512,3072]{1,0:T(8,128)(2,1)} %ck_ref.1, bf16[512,3072]{1,0:T(8,128)(2,1)} %cv_ref.1, s32[32,4]{1,0:T(8,128)} %copy.9.pattern_ref, s32[32]{0:T(128)} %reached_ref.1, ...), custom_call_target="tpu_custom_call" | custom-call | tf_op jit(solution)/shard_map/pallas_call | solution.py:347
  82.1 2.7 %copy.11 = bf16[128,6144]{1,0:T(8,128)(2,1)} copy(bf16[128,6144]{1,0:T(8,128)(2,1)} %shard_map.82) | data formatting | bytes 3145728
